TPU v7x, 256 devices: a whole 4x4x8 slice. The times are simulated.
256 devices in a mesh: tm: 64 (over y, z, core), space: 4 (over x).
Axes of the slice: x: 4, y: 4, z: 8, core: 2. Of those that a mesh axis runs over, the one named last changes fastest.
Arguments:
- latents: bfloat16 [1024, 2, 256, 128], P('tm', None, 'space'), may hold values from -6 to 6
- cotangent: bfloat16 [1024, 2, 256, 128], P('tm', None, 'space'), may hold values from -6 to 6
- clip_lengths: int32 [32], replicated, may hold values from 1 to 64, 1024 in all
- context_offset: int32 [32], replicated, may hold values from 0 to 63
- conv_weight: bfloat16 [3, 3, 128, 128], replicated, may hold values from -0.1875 to 0.1875
- w_query: bfloat16 [128, 128], replicated, may hold values from -0.5 to 0.5
- w_key: bfloat16 [128, 128], replicated, may hold values from -0.5 to 0.5
- w_value: bfloat16 [128, 128], replicated, may hold values from -0.5 to 0.5
- w_out: bfloat16 [128, 128], replicated, may hold values from -0.5 to 0.5
- query_gain: float32 [128], replicated, may hold values from 0.5 to 2
- key_gain: float32 [128], replicated, may hold values from 0.5 to 2
Outputs:
- outputs: bfloat16 [1024, 2, 256, 128], P('tm', None, 'space')
- latent_grad: bfloat16 [1024, 2, 256, 128], P('tm', None, 'space')
Inputs may be any that keep to these rules, and one draw needn't show every extreme that they name: `clip_lengths`: the clips cover the 1024 frames in order, one after another; some clip has exactly 64 frames.
All inputs are finite; a program needn't handle non-finite values.
Results may differ from a plain program's by a relative error of at most 0.0095.
Values may be sent and summed in bfloat16 or wider, within the bound.
A program may use at most 128 MiB of HBM per device.

v0:
```python
import jax
import jax.numpy as jnp
from jax import lax
from jax.experimental import pallas as pl
from jax.experimental.pallas import tpu as pltpu
from jax.sharding import PartitionSpec as P

HEAD = 64
SPAN = 4
GROUP = 4
HOPS = (-1, -2, -3, -4, 1, 2, 3, 4)
EPS = 1e-6
MESH = pl.DeviceIdType.MESH
VMEM = pltpu.VMEM
BF = jnp.bfloat16
F32 = jnp.float32
NT = (((1,), (1,)), ((), ()))
TN = (((0,), (0,)), ((), ()))


def dot(a, b):
    return jnp.dot(a, b, preferred_element_type=F32)


def dot_nt(a, b):
    return lax.dot_general(a, b, NT, preferred_element_type=F32)


def dot_tn(a, b):
    return lax.dot_general(a, b, TN, preferred_element_type=F32)


def partners():
    x, t = lax.axis_index("space"), lax.axis_index("tm")
    nx, nt = lax.axis_size("space"), lax.axis_size("tm")
    sides = [({"space": lax.rem(x + 1, nx)}, x + 1 < nx), ({"space": lax.rem(x + nx - 1, nx)}, x >= 1)]
    ups = [({"tm": lax.rem(t + k, nt)}, t + k < nt) for k in range(1, SPAN + 1)]
    downs = [({"tm": lax.rem(t + nt - k, nt)}, t >= k) for k in range(1, SPAN + 1)]
    return sides, ups, downs


class Message:
    def __init__(self, src, dst, send, recv, to, source):
        self.copy = pltpu.make_async_remote_copy(
            src_ref=src, dst_ref=dst, send_sem=send, recv_sem=recv, device_id=to[0], device_id_type=MESH
        )
        self.to, self.source = to[1], source[1]

    def start(self):
        pl.when(self.to)(self.copy.start)

    def sent(self):
        pl.when(self.to)(self.copy.wait_send)

    def arrived(self):
        pl.when(self.source)(self.copy.wait_recv)


def to_sides(src, dst, send, recv):
    sides, _, _ = partners()
    return [Message(src.at[i], dst.at[i], send.at[i], recv.at[i], sides[i], sides[1 - i]) for i in range(2)]


def to_clip(rising, falling, dst, send, recv):
    _, ups, downs = partners()
    out = []
    for k in reversed(range(SPAN)):
        j = SPAN + k
        out.append(Message(rising, dst.at[k], send.at[k], recv.at[k], ups[k], downs[k]))
        out.append(Message(falling, dst.at[j], send.at[j], recv.at[j], downs[k], ups[k]))
    return out


def build_conv(cw_ref, w3):
    for b in range(3):
        for rin in range(2):
            for rout in range(2):
                w3[
                    b * 256 + rin * 128 : b * 256 + rin * 128 + 128, rout * 128 : rout * 128 + 128
                ] = cw_ref[rin - rout + 1, b]


def joined(ref, f):
    return jnp.concatenate([ref[f, 0:64, :], ref[f, 64:128, :]], axis=1).astype(F32)


def shifted(x, left, right):
    row = lax.broadcasted_iota(jnp.int32, (64, 1), 0)
    before = jnp.where(row == 0, left, pltpu.roll(x, 1, 0))
    after = jnp.where(row == 63, right, pltpu.roll(x, 63, 0))
    return before.astype(BF), x.astype(BF), after.astype(BF)


def conv(xs, w3):
    taps = [jnp.concatenate(shifted(*x), axis=1) for x in xs]
    taps = jnp.concatenate(taps, axis=0) if len(taps) > 1 else taps[0]
    whole = jnp.concatenate([x[0] for x in xs], axis=0) if len(xs) > 1 else xs[0][0]
    return whole + dot(taps, w3[...])


def conv_back(xs, w3):
    parts = [shifted(*x) for x in xs]
    cat = lambda i: jnp.concatenate([p[i] for p in parts], axis=0) if len(parts) > 1 else parts[0][i]
    whole = jnp.concatenate([x[0] for x in xs], axis=0) if len(xs) > 1 else xs[0][0]
    out = dot_nt(cat(0), w3[512:768, :])
    out = out + dot_nt(cat(1), w3[256:512, :])
    out = out + dot_nt(cat(2), w3[0:256, :])
    return whole + out


def put(ref, f, y):
    ref[f, 0:64, :] = y[:, :128].astype(ref.dtype)
    ref[f, 64:128, :] = y[:, 128:].astype(ref.dtype)


def edges_out(ref, f, edges, at):
    x = joined(ref, f)
    edges[0, pl.ds(at, 1), :] = x[63:64]
    edges[1, pl.ds(at, 1), :] = x[0:1]


def mask_edges(halo):
    x, nx = lax.axis_index("space"), lax.axis_size("space")
    halo[0] = jnp.where(x > 0, halo[0], 0.0)
    halo[1] = jnp.where(x < nx - 1, halo[1], 0.0)


def halo_rows(halo, f):
    return halo[0, pl.ds(f, 1), :], halo[1, pl.ds(f, 1), :]


def with_halo(ref, halo, f):
    return (joined(ref, f), *halo_rows(halo, f))


def cells(y):
    parts = []
    for i in range(y.shape[0] // 64):
        parts += [y[i * 64 : i * 64 + 64, :128], y[i * 64 : i * 64 + 64, 128:]]
    return jnp.concatenate(parts, axis=0)


def block_ones(rows, cols, rblock, cblock, value):
    r = lax.broadcasted_iota(jnp.int32, (rows, cols), 0) // rblock
    c = lax.broadcasted_iota(jnp.int32, (rows, cols), 1) // cblock
    return jnp.where(r == c, value, 0.0).astype(BF)


def kernel(
    lens_h, offs_h, lat_h, ct_h, cw_h, wq_h, wk_h, wv_h, wo_h, qg_h, kg_h, out, lg,
    lens, offs, starts, targets, slots, lastf,
    lat, ct, cw, wq, wk, wv, wo, qg, kg,
    w3, wqk, wvo, wqkt, wvot,
    hid, qs, un, sc, kk, vv, ga, gq, att, dk, dv, gh, base,
    edge_f, halo_f, ctx_f, rim_f, got_f, gotrim_f,
    edge_b, halo_b, edge_g, halo_g, ctx_b, rim_b, got_b, gotrim_b,
    load_sem, side_send, side_recv, clip_send, clip_recv,
):
    frames = lat.shape[0]
    t, nt = lax.axis_index("tm"), lax.axis_size("tm")
    first = t * frames
    last = first + frames - 1

    pairs = [
        (lens_h, lens), (offs_h, offs), (lat_h, lat), (cw_h, cw), (ct_h, ct), (wq_h, wq), (wk_h, wk),
        (wv_h, wv), (wo_h, wo), (qg_h, qg), (kg_h, kg),
    ]
    loads = [pltpu.make_async_copy(a, b, load_sem.at[i]) for i, (a, b) in enumerate(pairs)]
    for c in loads:
        c.start()
    sides, ups, downs = partners()
    barrier = pltpu.get_barrier_semaphore()
    for who, there in sides + ups + downs:

        @pl.when(there)
        def _(who=who):
            pl.semaphore_signal(barrier, inc=1, device_id=who, device_id_type=MESH)

    loads[0].wait()
    loads[1].wait()

    def scan(j, c):
        start, top, low, below, below_end, above = c
        length = lens[j]
        end = start + length
        target = start + lax.rem(offs[j], length)
        starts[j] = start
        targets[j] = target
        inside = (target >= first) & (target <= last)
        top = jnp.where(inside, target, top)
        low = jnp.where(inside, jnp.minimum(low, target), low)
        at_first = start <= first
        below = jnp.where(at_first, target, below)
        below_end = jnp.where(at_first, end, below_end)
        above = jnp.where(start <= last, target, above)
        return end, top, low, below, below_end, above

    init = (jnp.int32(0), first, last, first, first, last)
    _, top, low, below, below_end, above = lax.fori_loop(0, lens.shape[0], scan, init, unroll=4)
    top, low = top - first, low - first
    up_at = jnp.clip((first - below + frames - 1) // frames, 1, SPAN) - 1
    down_at = jnp.clip((above - first) // frames, 1, SPAN) - 1 + SPAN

    loads[2].wait()
    ctx_f[0] = lat[top]
    ctx_f[1] = lat[low]
    for f in range(frames):
        edges_out(lat, f, edge_f, f)
    pl.semaphore_wait(barrier, sum(there.astype(jnp.int32) for _, there in sides + ups + downs))

    halos_f = to_sides(edge_f, halo_f, side_send.at[0], side_recv.at[0])
    frames_f = to_clip(ctx_f.at[0], ctx_f.at[1], got_f, clip_send.at[0], clip_recv.at[0])
    rims_f = to_clip(rim_f.at[0], rim_f.at[1], gotrim_f, clip_send.at[1], clip_recv.at[1])
    for m in halos_f + frames_f:
        m.start()

    def scan2(j, c):
        slot, lastof, near = c
        start, target = starts[j], targets[j]
        at = target - first
        mine = jnp.where(at < 0, frames, jnp.where(at >= frames, frames + 1, at))
        end = jnp.minimum(start + lens[j] - 1, last) - first
        slot = [jnp.where(start - first <= f, mine, s) for f, s in enumerate(slot)]
        lastof = [jnp.where(at == f, end, s) for f, s in enumerate(lastof)]
        near = [
            jnp.where(start <= (first + k * frames if k > 0 else last + k * frames), target, s)
            for k, s in zip(HOPS, near)
        ]
        return slot, lastof, near

    zero = jnp.int32(0)
    slot, lastof, near = lax.fori_loop(
        0, lens.shape[0], scan2, ([zero] * frames, [zero - 1] * frames, [zero - 1] * len(HOPS)), unroll=2
    )
    for f in range(frames):
        slots[f] = slot[f]
        lastf[f] = lastof[f]
    lastf[frames] = jnp.where(below < first, jnp.minimum(below_end - 1, last) - first, -1)
    lastf[frames + 1] = jnp.where(above > last, frames - 1, -1)
    hits = [
        (near[i] >= first) & (near[i] <= last) & ((t + k < nt) if k > 0 else (t + k >= 0))
        for i, k in enumerate(HOPS)
    ]

    for c in loads[3:]:
        c.wait()
    build_conv(cw, w3)
    none = jnp.zeros((128, 128), BF)
    wqk[:, :128] = wq[...]
    wqk[:, 128:] = wk[...]
    wvo[:128, :128] = wv[...]
    wvo[:128, 128:] = none
    wvo[128:, :128] = none
    wvo[128:, 128:] = wo[...].astype(F32).T.astype(BF)
    wqkt[:128, :] = wq[...].astype(F32).T.astype(BF)
    wqkt[128:, :] = wk[...].astype(F32).T.astype(BF)
    wvot[:128, :128] = wv[...].astype(F32).T.astype(BF)
    wvot[:128, 128:] = none
    wvot[128:, :128] = none
    wvot[128:, 128:] = wo[...]
    mean4 = block_ones(256, 256, HEAD, HEAD, 1.0 / HEAD)
    ones2 = block_ones(256, 256, 128, 128, 1.0)
    spread = block_ones(128, 256, HEAD, 128, 1.0)
    gains = jnp.concatenate([qg[...], kg[...]], axis=1)
    head0 = lax.broadcasted_iota(jnp.int32, (1, 128), 1) < HEAD
    dk[0] = jnp.zeros((128, 128), F32)
    dv[0] = jnp.zeros((128, 128), F32)

    for m in halos_f:
        m.arrived()
    mask_edges(halo_f)
    for i, f in enumerate((top, low)):
        left, right = halo_rows(halo_f, f)
        rim_f[i, 0:1] = left
        rim_f[i, 1:2] = right
    for m in rims_f:
        m.start()

    def project(h, c, at, real):
        qk = dot(h, wqk[...])
        vg = dot(jnp.concatenate([h, c], axis=1), wvo[...])
        s = lax.rsqrt(dot((qk * qk).astype(BF), mean4) + EPS)
        u = qk * s
        y = u * gains
        for i in range(h.shape[0] // 128):
            rows = slice(i * 128, i * 128 + 128)
            f = at + i
            un[f] = u[rows]
            sc[f] = s[rows]
            key, val = y[rows, 128:], vg[rows, :128]
            kk[f, :128] = jnp.where(head0, key, 0.0).astype(BF)
            kk[f, 128:] = jnp.where(head0, 0.0, key).astype(BF)
            vv[f, :128] = jnp.where(head0, val, 0.0).astype(BF)
            vv[f, 128:] = jnp.where(head0, 0.0, val).astype(BF)
            if real:
                qs[f] = y[rows, :128].astype(BF)
                ga[f] = vg[rows, 128:].astype(BF)

    @pl.loop(0, frames // 2)
    def _(g):
        h = cells(conv([with_halo(lat, halo_f, g * 2 + i) for i in range(2)], w3).astype(BF))
        at = pl.ds(g * 2, 2)
        hid[at] = h.reshape(2, 128, 128)
        project(h, ct[at].reshape(256, 128), g * 2, True)

    for m in frames_f + rims_f:
        m.arrived()
    below_there, above_there = t > 0, t < nt - 1
    far = []
    for at, there in ((up_at, below_there), (down_at, above_there)):
        x = jnp.where(there, joined(got_f, at), 0.0)
        rim = jnp.where(there, gotrim_f[at], 0.0)
        far.append((x, rim[0:1], rim[1:2]))
    both = cells(conv(far, w3).astype(BF))
    project(both, both, frames, False)

    @pl.loop(0, frames // GROUP)
    def _(g):
        at = [g * GROUP + i for i in range(GROUP)]
        slot = [slots[f] for f in at]
        same = [slots[jnp.maximum(f - 1, 0)] == s for f, s in zip(at, slot)]
        n = range(GROUP)
        raised = [jnp.exp(dot_nt(qs[at[i]], kk[slot[i]]) * 0.125) for i in n]
        total = [dot(r.astype(BF), ones2) for r in raised]
        prob = [raised[i] / total[i] for i in n]
        low_p = [p.astype(BF) for p in prob]
        o = [dot(low_p[i], vv[slot[i]]) for i in n]
        gp = [dot_nt(ga[at[i]], vv[slot[i]]) for i in n]
        for i in n:
            att[at[i]] = o[i].astype(BF)
        delta = [dot((o[i] * ga[at[i]].astype(F32)).astype(BF), spread) for i in n]
        ds = [(prob[i] * (gp[i] - delta[i]) * 0.125).astype(BF) for i in n]
        for i in n:
            gq[at[i]] = dot(ds[i], kk[slot[i]])
        kt = [dot_tn(qs[at[i]], ds[i]) for i in n]
        vt = [dot_tn(ga[at[i]], low_p[i]) for i in n]
        for acc, terms in ((dk, kt), (dv, vt)):
            run = acc[g * GROUP]
            for i in n:
                term = jnp.concatenate([terms[i][:64, :128], terms[i][64:, 128:]], axis=0)
                run = jnp.where(same[i], run, 0.0) + term
                acc[at[i] + 1] = run

    def finish(at, real):
        rows, vals = [], []
        for i in range(2):
            f = at + i
            left = gq[f] if real else jnp.zeros((128, 128), F32)
            until = jnp.clip(lastf[f] + 1, 0, frames)
            rows.append(jnp.concatenate([left, dk[until].T], axis=1))
            vals.append(dv[until].T)
        e = jnp.concatenate(rows, axis=0) * gains
        u = jnp.concatenate([un[at], un[at + 1]], axis=0)
        s = jnp.concatenate([sc[at], sc[at + 1]], axis=0)
        m = dot((e * u).astype(BF), mean4)
        raw = (s * (e - u * m)).astype(BF)
        val = jnp.concatenate(vals, axis=0).astype(BF)
        a = jnp.concatenate([att[at], att[at + 1]], axis=0) if real else val
        back = dot(raw, wqkt[...])
        vo = dot(jnp.concatenate([val, a], axis=1), wvot[...])
        return back + vo[:, :128], vo[:, 128:]

    def finish_local(g):
        back, o = finish(g * 2, True)
        at = pl.ds(g * 2, 2)
        out[at] = (hid[at].astype(F32) + o.reshape(2, 128, 128)).astype(BF)
        gh[at] = (ct[at].astype(F32) + back.reshape(2, 128, 128)).astype(BF)

    owed, _ = finish(frames, False)
    ctx_b[...] = owed.reshape(2, 128, 128).astype(BF)
    for i in range(2):
        edges_out(ctx_b, i, edge_g, i)
    frames_b = to_clip(ctx_b.at[1], ctx_b.at[0], got_b, clip_send.at[2], clip_recv.at[2])
    rims_b = to_clip(rim_b.at[1], rim_b.at[0], gotrim_b, clip_send.at[3], clip_recv.at[3])
    halos_g = to_sides(edge_g, halo_g, side_send.at[1], side_recv.at[1])
    halos_b = to_sides(edge_b, halo_b, side_send.at[2], side_recv.at[2])
    for m in halos_g + frames_b:
        m.start()
    pl.loop(0, frames // 2)(finish_local)
    for f in range(frames):
        edges_out(gh, f, edge_b, f)
    for m in halos_b:
        m.start()
    for m in halos_g:
        m.arrived()
    mask_edges(halo_g)
    for i in range(2):
        left, right = halo_rows(halo_g, i)
        rim_b[i, 0:1] = left
        rim_b[i, 1:2] = right
    for m in rims_b:
        m.start()
    for m in halos_b:
        m.arrived()
    mask_edges(halo_b)

    @pl.loop(0, frames // GROUP)
    def _(g):
        y = conv_back([with_halo(gh, halo_b, g * GROUP + i) for i in range(GROUP)], w3)
        for i in range(GROUP):
            put(base, g * GROUP + i, y[i * 64 : i * 64 + 64])

    for m in frames_b + rims_b:
        m.arrived()
    sums = []
    for at in (SPAN, 0):
        x, rim = jnp.zeros((64, 256), F32), jnp.zeros((2, 256), F32)
        for k in range(SPAN):
            x += jnp.where(hits[at + k], joined(got_b, at + k), 0.0)
            rim += jnp.where(hits[at + k], gotrim_b[at + k], 0.0)
        sums.append((x, rim[0:1], rim[1:2]))
    pair = cells(conv_back(sums, w3))
    for_top, for_low = pair[:128], pair[128:]

    @pl.loop(0, frames)
    def _(f):
        y = base[f] + jnp.where(f == top, for_top, 0.0) + jnp.where(f == low, for_low, 0.0)
        lg[f] = y.astype(BF)

    for m in halos_f + frames_f + rims_f + halos_g + frames_b + rims_b + halos_b:
        m.sent()


def per_device(
    latents, cotangent, clip_lengths, context_offset, conv_weight, w_query, w_key, w_value, w_out, query_gain, key_gain
):
    frames, rows, width, channels = latents.shape
    flat = (frames, rows * width, channels)
    one = (rows * width, channels)
    square = (channels, channels)
    slots = frames + 2
    clips = clip_lengths.shape[0]
    smem = lambda n: pltpu.SMEM((n,), jnp.int32)
    edge, few = VMEM((2, frames, 256), F32), VMEM((2, 8, 256), F32)
    comm = lambda: [VMEM((2, *one), BF), VMEM((2, 2, 256), F32), VMEM((2 * SPAN, *one), BF), VMEM((2 * SPAN, 2, 256), F32)]
    result = jax.ShapeDtypeStruct(flat, BF)
    out, lg = pl.pallas_call(
        kernel,
        name="tokenizer_block",
        out_shape=(result, result),
        in_specs=[pl.BlockSpec(memory_space=pltpu.HBM)] * 11,
        out_specs=(pl.BlockSpec(memory_space=VMEM),) * 2,
        scratch_shapes=[smem(clips)] * 4
        + [smem(frames), smem(slots)]
        + [VMEM(flat, BF), VMEM(flat, BF), VMEM(conv_weight.shape, BF)]
        + [VMEM(square, BF)] * 4
        + [VMEM((1, channels), F32)] * 2
        + [VMEM((768, 256), BF), VMEM((128, 256), BF), VMEM((256, 256), BF), VMEM((256, 128), BF), VMEM((256, 256), BF)]
        + [
            VMEM(flat, BF),
            VMEM(flat, BF),
            VMEM((slots, 128, 256), F32),
            VMEM((slots, 128, 256), F32),
            VMEM((slots, 256, 128), BF),
            VMEM((slots, 256, 128), BF),
            VMEM(flat, BF),
            VMEM(flat, F32),
            VMEM(flat, BF),
            VMEM((frames + 1, 128, 128), F32),
            VMEM((frames + 1, 128, 128), F32),
            VMEM(flat, BF),
            VMEM(flat, F32),
        ]
        + [edge, edge]
        + comm()
        + [edge, edge, few, few]
        + comm()
        + [
            pltpu.SemaphoreType.DMA((11,)),
            pltpu.SemaphoreType.DMA((3, 2)),
            pltpu.SemaphoreType.DMA((3, 2)),
            pltpu.SemaphoreType.DMA((4, 2 * SPAN)),
            pltpu.SemaphoreType.DMA((4, 2 * SPAN)),
        ],
        compiler_params=pltpu.CompilerParams(
            collective_id=0, has_side_effects=True, vmem_limit_bytes=40 << 20
        ),
    )(
        clip_lengths, context_offset, latents.reshape(flat), cotangent.reshape(flat), conv_weight,
        w_query, w_key, w_value, w_out, query_gain.reshape(1, channels), key_gain.reshape(1, channels),
    )
    return out.reshape(latents.shape), lg.reshape(latents.shape)


def solution(mesh):
    data = P("tm", None, "space", None)
    return jax.shard_map(
        per_device,
        mesh=mesh,
        in_specs=(data, data) + (P(),) * 9,
        out_specs=(data, data),
        check_vma=False,
    )
```

profile of v0, /device:TPU:24, one launch (start us, length us, event | category | flops | bytes accessed | tf_op | source)
XLA Modules:
  0.0 37.3 jit_solution(14869923621110725085)
XLA Ops:
  0.6 0.0 copy-start.10
  0.6 0.0 copy-start.7
  0.7 0.0 copy-start.8
  0.7 0.0 copy-start.9
  0.7 0.6 %copy-done.10 = f32[128]{0:T(128)S(1)} copy-done((f32[128]{0:T(128)S(1)}, f32[128]{0:T(128)}, u32[]{:S(2)}) %copy-start.10) | copy-done | bytes 536
  1.3 0.0 copy-done.7
  1.3 0.0 copy-done.8
  1.3 0.0 copy-done.9
  1.3 0.0 copy-start
  1.3 1.0 %copy-done = bf16[16,2,64,128]{3,2,1,0:T(8,128)(2,1)S(1)} copy-done((bf16[16,2,64,128]{3,2,1,0:T(8,128)(2,1)S(1)}, bf16[16,2,64,128]{3,2,1,0:T(8,128)(2,1)}, u32[]{:S(2)}) %copy-start) | copy-done | bytes 524312
  2.4 0.0 copy-start.1
  2.4 1.0 %copy-done.1 = bf16[16,2,64,128]{3,2,1,0:T(8,128)(2,1)S(1)} copy-done((bf16[16,2,64,128]{3,2,1,0:T(8,128)(2,1)S(1)}, bf16[16,2,64,128]{3,2,1,0:T(8,128)(2,1)}, u32[]{:S(2)}) %copy-start.1) | copy-done | bytes 524312
  3.4 0.0 copy-start.2
  3.4 1.0 %copy-done.2 = bf16[3,3,128,128]{3,2,1,0:T(8,128)(2,1)S(1)} copy-done((bf16[3,3,128,128]{3,2,1,0:T(8,128)(2,1)S(1)}, bf16[3,3,128,128]{3,2,1,0:T(8,128)(2,1)}, u32[]{:S(2)}) %copy-start.2) | copy-done | bytes 294936
  4.4 0.0 copy-start.3
  4.4 0.8 %copy-done.3 = bf16[128,128]{1,0:T(8,128)(2,1)S(1)} copy-done((bf16[128,128]{1,0:T(8,128)(2,1)S(1)}, bf16[128,128]{1,0:T(8,128)(2,1)}, u32[]{:S(2)}) %copy-start.3) | copy-done | bytes 32792
  5.1 0.0 copy-start.4
  5.1 0.8 %copy-done.4 = bf16[128,128]{1,0:T(8,128)(2,1)S(1)} copy-done((bf16[128,128]{1,0:T(8,128)(2,1)S(1)}, bf16[128,128]{1,0:T(8,128)(2,1)}, u32[]{:S(2)}) %copy-start.4) | copy-done | bytes 32792
  5.9 0.0 copy-start.5
  5.9 0.8 %copy-done.5 = bf16[128,128]{1,0:T(8,128)(2,1)S(1)} copy-done((bf16[128,128]{1,0:T(8,128)(2,1)S(1)}, bf16[128,128]{1,0:T(8,128)(2,1)}, u32[]{:S(2)}) %copy-start.5) | copy-done | bytes 32792
  6.7 0.8 %copy-done.6 = bf16[128,128]{1,0:T(8,128)(2,1)S(1)} copy-done((bf16[128,128]{1,0:T(8,128)(2,1)S(1)}, bf16[128,128]{1,0:T(8,128)(2,1)}, u32[]{:S(2)}) %copy-start.6) | copy-done | bytes 32792
  7.4 28.3 %tokenizer_block.1 = (bf16[16,128,128]{2,1,0:T(8,128)(2,1)S(1)}, bf16[16,128,128]{2,1,0:T(8,128)(2,1)S(1)}) custom-call(s32[32]{0:T(128)S(1)} %copy-done.7, s32[32]{0:T(128)S(1)} %copy-done.8, bf16[16,128,128]{2,1,0:T(8,128)(2,1)S(1)} %bitcast.6, bf16[16,128,128]{2,1,0:T(8,128)(2,1)S(1)} %bitcast.7, bf16[3,3,128,128]{3,2,1,0:T(8,128)(2,1)S(1)} %copy-done.2, ...), custom_call_target="tpu_custom_call" | custom-call | tf_op jit(solution)/shard_map/tokenizer_block/pallas_call | solution.py:437
  35.7 0.8 %copy.15 = bf16[16,2,64,128]{3,2,1,0:T(8,128)(2,1)} copy(bf16[16,2,64,128]{3,2,1,0:T(8,128)(2,1)S(1)} %bitcast.9) | data formatting | bytes 1048576
  36.5 0.8 %copy.16 = bf16[16,2,64,128]{3,2,1,0:T(8,128)(2,1)} copy(bf16[16,2,64,128]{3,2,1,0:T(8,128)(2,1)S(1)} %bitcast.8) | data formatting | bytes 1048576
  (1 shorter events, 0.0 us)
Async XLA Ops:
  0.6 0.7 %copy-start.10 = (f32[128]{0:T(128)S(1)}, f32[128]{0:T(128)}, u32[]{:S(2)}) copy-start(f32[128]{0:T(128)} %param.21) | copy-start | bytes 1540
  0.6 0.7 %copy-start.7 = (s32[32]{0:T(128)S(1)}, s32[32]{0:T(128)}, u32[]{:S(2)}) copy-start(s32[32]{0:T(128)} %lens_h.1) | copy-start | bytes 388
  0.7 0.7 %copy-start.8 = (s32[32]{0:T(128)S(1)}, s32[32]{0:T(128)}, u32[]{:S(2)}) copy-start(s32[32]{0:T(128)} %offs_h.1) | copy-start | bytes 388
  0.7 0.7 %copy-start.9 = (f32[128]{0:T(128)S(1)}, f32[128]{0:T(128)}, u32[]{:S(2)}) copy-start(f32[128]{0:T(128)} %param.20) | copy-start | bytes 1540
  1.3 1.0 %copy-start = (bf16[16,2,64,128]{3,2,1,0:T(8,128)(2,1)S(1)}, bf16[16,2,64,128]{3,2,1,0:T(8,128)(2,1)}, u32[]{:S(2)}) copy-start(bf16[16,2,64,128]{3,2,1,0:T(8,128)(2,1)} %param.11) | copy-start | bytes 1572868
  2.4 1.0 %copy-start.1 = (bf16[16,2,64,128]{3,2,1,0:T(8,128)(2,1)S(1)}, bf16[16,2,64,128]{3,2,1,0:T(8,128)(2,1)}, u32[]{:S(2)}) copy-start(bf16[16,2,64,128]{3,2,1,0:T(8,128)(2,1)} %param.12) | copy-start | bytes 1572868
  3.4 1.0 %copy-start.2 = (bf16[3,3,128,128]{3,2,1,0:T(8,128)(2,1)S(1)}, bf16[3,3,128,128]{3,2,1,0:T(8,128)(2,1)}, u32[]{:S(2)}) copy-start(bf16[3,3,128,128]{3,2,1,0:T(8,128)(2,1)} %cw_h.1) | copy-start | bytes 884740
  4.4 0.8 %copy-start.3 = (bf16[128,128]{1,0:T(8,128)(2,1)S(1)}, bf16[128,128]{1,0:T(8,128)(2,1)}, u32[]{:S(2)}) copy-start(bf16[128,128]{1,0:T(8,128)(2,1)} %wq_h.1) | copy-start | bytes 98308
  5.1 0.8 %copy-start.4 = (bf16[128,128]{1,0:T(8,128)(2,1)S(1)}, bf16[128,128]{1,0:T(8,128)(2,1)}, u32[]{:S(2)}) copy-start(bf16[128,128]{1,0:T(8,128)(2,1)} %wk_h.1) | copy-start | bytes 98308
  5.9 0.8 %copy-start.5 = (bf16[128,128]{1,0:T(8,128)(2,1)S(1)}, bf16[128,128]{1,0:T(8,128)(2,1)}, u32[]{:S(2)}) copy-start(bf16[128,128]{1,0:T(8,128)(2,1)} %wv_h.1) | copy-start | bytes 98308
  6.7 0.8 %copy-start.6 = (bf16[128,128]{1,0:T(8,128)(2,1)S(1)}, bf16[128,128]{1,0:T(8,128)(2,1)}, u32[]{:S(2)}) copy-start(bf16[128,128]{1,0:T(8,128)(2,1)} %wo_h.1) | copy-start | bytes 98308
where the time goes:
time: 37.8 us; the launch traced here: 37.3 us
  Pallas kernels  28.3 us (75%)
  local copies, waits for them, and re-layouts  8.33 us (22%)
  between operations  0.68 us (2%)
    pallas_call x1, Pallas kernels, per_device(): pl.pallas_call(kernel, name='tokenizer_block', out_shape=(result, result)...  28.3 us
    unnamed x24, local copies, waits for them, and re-layouts  8.33 us

commit v1 on v0

--- a/solution.py
+++ b/solution.py
@@ -147,14 +147,14 @@
 
 
 def kernel(
-    lens_h, offs_h, lat_h, ct_h, cw_h, wq_h, wk_h, wv_h, wo_h, qg_h, kg_h, out, lg,
+    lens_h, offs_h, lat_h, ct_h, cw_h, wq_h, wk_h, wv_h, wo_h, qg_h, kg_h, out_h, lg_h, pair_h, spot_h,
     lens, offs, starts, targets, slots, lastf,
     lat, ct, cw, wq, wk, wv, wo, qg, kg,
-    w3, wqk, wvo, wqkt, wvot,
-    hid, qs, un, sc, kk, vv, ga, gq, att, dk, dv, gh, base,
+    w3, wqk, wvo, wqkt, wvt,
+    hid, qs, un, sc, kk, vv, ga, gq, att, dk, dv, gh,
     edge_f, halo_f, ctx_f, rim_f, got_f, gotrim_f,
     edge_b, halo_b, edge_g, halo_g, ctx_b, rim_b, got_b, gotrim_b,
-    load_sem, side_send, side_recv, clip_send, clip_recv,
+    conv_f, rims, out, lg, pair, spot, load_sem, store_sem, side_send, side_recv, clip_send, clip_recv,
 ):
     frames = lat.shape[0]
     t, nt = lax.axis_index("tm"), lax.axis_size("tm")
@@ -198,6 +198,10 @@
     init = (jnp.int32(0), first, last, first, first, last)
     _, top, low, below, below_end, above = lax.fori_loop(0, lens.shape[0], scan, init, unroll=4)
     top, low = top - first, low - first
+    spot[0] = top
+    spot[1] = low
+    spots = pltpu.make_async_copy(spot, spot_h, store_sem.at[3])
+    spots.start()
     up_at = jnp.clip((first - below + frames - 1) // frames, 1, SPAN) - 1
     down_at = jnp.clip((above - first) // frames, 1, SPAN) - 1 + SPAN
 
@@ -254,10 +258,7 @@
     wvo[128:, 128:] = wo[...].astype(F32).T.astype(BF)
     wqkt[:128, :] = wq[...].astype(F32).T.astype(BF)
     wqkt[128:, :] = wk[...].astype(F32).T.astype(BF)
-    wvot[:128, :128] = wv[...].astype(F32).T.astype(BF)
-    wvot[:128, 128:] = none
-    wvot[128:, :128] = none
-    wvot[128:, 128:] = wo[...]
+    wvt[...] = wv[...].astype(F32).T.astype(BF)
     mean4 = block_ones(256, 256, HEAD, HEAD, 1.0 / HEAD)
     ones2 = block_ones(256, 256, 128, 128, 1.0)
     spread = block_ones(128, 256, HEAD, 128, 1.0)
@@ -265,6 +266,14 @@
     head0 = lax.broadcasted_iota(jnp.int32, (1, 128), 1) < HEAD
     dk[0] = jnp.zeros((128, 128), F32)
     dv[0] = jnp.zeros((128, 128), F32)
+
+    edgeless = jnp.zeros((1, 256), F32)
+
+    @pl.loop(0, frames // GROUP)
+    def _(g):
+        y = conv([(joined(lat, g * GROUP + i), edgeless, edgeless) for i in range(GROUP)], w3)
+        for i in range(GROUP):
+            conv_f[g * GROUP + i] = y[i * 64 : i * 64 + 64]
 
     for m in halos_f:
         m.arrived()
@@ -275,6 +284,11 @@
         rim_f[i, 1:2] = right
     for m in rims_f:
         m.start()
+    left = dot(halo_f[0].astype(BF), w3[0:256, :])
+    right = dot(halo_f[1].astype(BF), w3[512:768, :])
+    for f in range(frames):
+        conv_f[f, 0:1, :] += left[f : f + 1]
+        conv_f[f, 63:64, :] += right[f : f + 1]
 
     def project(h, c, at, real):
         qk = dot(h, wqk[...])
@@ -298,7 +312,7 @@
 
     @pl.loop(0, frames // 2)
     def _(g):
-        h = cells(conv([with_halo(lat, halo_f, g * 2 + i) for i in range(2)], w3).astype(BF))
+        h = cells(jnp.concatenate([conv_f[g * 2], conv_f[g * 2 + 1]], axis=0).astype(BF))
         at = pl.ds(g * 2, 2)
         hid[at] = h.reshape(2, 128, 128)
         project(h, ct[at].reshape(256, 128), g * 2, True)
@@ -355,19 +369,13 @@
         m = dot((e * u).astype(BF), mean4)
         raw = (s * (e - u * m)).astype(BF)
         val = jnp.concatenate(vals, axis=0).astype(BF)
-        a = jnp.concatenate([att[at], att[at + 1]], axis=0) if real else val
-        back = dot(raw, wqkt[...])
-        vo = dot(jnp.concatenate([val, a], axis=1), wvot[...])
-        return back + vo[:, :128], vo[:, 128:]
+        return dot(raw, wqkt[...]) + dot(val, wvt[...])
 
     def finish_local(g):
-        back, o = finish(g * 2, True)
         at = pl.ds(g * 2, 2)
-        out[at] = (hid[at].astype(F32) + o.reshape(2, 128, 128)).astype(BF)
-        gh[at] = (ct[at].astype(F32) + back.reshape(2, 128, 128)).astype(BF)
-
-    owed, _ = finish(frames, False)
-    ctx_b[...] = owed.reshape(2, 128, 128).astype(BF)
+        gh[at] = (ct[at].astype(F32) + finish(g * 2, True).reshape(2, 128, 128)).astype(BF)
+
+    ctx_b[...] = finish(frames, False).reshape(2, 128, 128).astype(BF)
     for i in range(2):
         edges_out(ctx_b, i, edge_g, i)
     frames_b = to_clip(ctx_b.at[1], ctx_b.at[0], got_b, clip_send.at[2], clip_recv.at[2])
@@ -390,16 +398,43 @@
         rim_b[i, 1:2] = right
     for m in rims_b:
         m.start()
+
+    @pl.loop(0, frames // GROUP)
+    def _(g):
+        at = pl.ds(g * GROUP, GROUP)
+        o = dot(att[at].reshape(GROUP * 128, 128), wo[...])
+        out[at] = (hid[at].astype(F32) + o.reshape(GROUP, 128, 128)).astype(BF)
+
+    stores = [pltpu.make_async_copy(out, out_h, store_sem.at[0])]
+    stores[0].start()
+
+    @pl.loop(0, frames // GROUP)
+    def _(g):
+        y = conv_back([(joined(gh, g * GROUP + i), edgeless, edgeless) for i in range(GROUP)], w3)
+        for i in range(GROUP):
+            f = g * GROUP + i
+            put(lg, f, y[i * 64 : i * 64 + 64])
+            rims[0, pl.ds(f, 1), :] = y[i * 64 : i * 64 + 1]
+            rims[1, pl.ds(f, 1), :] = y[i * 64 + 63 : i * 64 + 64]
+
     for m in halos_b:
         m.arrived()
     mask_edges(halo_b)
-
-    @pl.loop(0, frames // GROUP)
-    def _(g):
-        y = conv_back([with_halo(gh, halo_b, g * GROUP + i) for i in range(GROUP)], w3)
-        for i in range(GROUP):
-            put(base, g * GROUP + i, y[i * 64 : i * 64 + 64])
-
+    rims[0] += dot_nt(halo_b[0].astype(BF), w3[512:768, :])
+    rims[1] += dot_nt(halo_b[1].astype(BF), w3[0:256, :])
+    row = lax.broadcasted_iota(jnp.int32, (16, 1), 0)
+
+    @pl.loop(0, frames)
+    def _(f):
+        for side, start, at in ((0, 0, 0), (1, 48, 15)):
+            edge = rims[side, pl.ds(f, 1), :]
+            for r in range(2):
+                rows = slice(r * 64 + start, r * 64 + start + 16)
+                tile = jnp.where(row == at, edge[:, r * 128 : r * 128 + 128], lg[f, rows, :].astype(F32))
+                lg[f, rows, :] = tile.astype(BF)
+
+    stores.append(pltpu.make_async_copy(lg, lg_h, store_sem.at[1]))
+    stores[1].start()
     for m in frames_b + rims_b:
         m.arrived()
     sums = []
@@ -409,16 +444,31 @@
             x += jnp.where(hits[at + k], joined(got_b, at + k), 0.0)
             rim += jnp.where(hits[at + k], gotrim_b[at + k], 0.0)
         sums.append((x, rim[0:1], rim[1:2]))
-    pair = cells(conv_back(sums, w3))
-    for_top, for_low = pair[:128], pair[128:]
-
-    @pl.loop(0, frames)
-    def _(f):
-        y = base[f] + jnp.where(f == top, for_top, 0.0) + jnp.where(f == low, for_low, 0.0)
-        lg[f] = y.astype(BF)
-
+    pair[...] = cells(conv_back(sums, w3)).reshape(2, 128, 128)
+    stores.append(pltpu.make_async_copy(pair, pair_h, store_sem.at[2]))
+    stores[2].start()
+    for c in stores + [spots]:
+        c.wait()
     for m in halos_f + frames_f + rims_f + halos_g + frames_b + rims_b + halos_b:
         m.sent()
+
+
+def hand_over(out_k, lg_k, pair_k, spot_k, out_h, lg_h, out, lg, pair, spot, load, store):
+    moves = ((out_k, out, out_h), (lg_k, lg, lg_h), (pair_k, pair, None), (spot_k, spot, None))
+    loads = [pltpu.make_async_copy(a, b, load.at[i]) for i, (a, b, _) in enumerate(moves)]
+    stores = [pltpu.make_async_copy(b, c, store.at[i]) for i, (_, b, c) in enumerate(moves[:2])]
+    for c in loads:
+        c.start()
+    loads[0].wait()
+    stores[0].start()
+    for c in loads[1:]:
+        c.wait()
+    for i in range(2):
+        at = spot[i]
+        lg[at] = (lg[at].astype(F32) + pair[i]).astype(BF)
+    stores[1].start()
+    for c in stores:
+        c.wait()
 
 
 def per_device(
@@ -434,18 +484,18 @@
     edge, few = VMEM((2, frames, 256), F32), VMEM((2, 8, 256), F32)
     comm = lambda: [VMEM((2, *one), BF), VMEM((2, 2, 256), F32), VMEM((2 * SPAN, *one), BF), VMEM((2 * SPAN, 2, 256), F32)]
     result = jax.ShapeDtypeStruct(flat, BF)
-    out, lg = pl.pallas_call(
+    out, lg, pair, spot = pl.pallas_call(
         kernel,
         name="tokenizer_block",
-        out_shape=(result, result),
+        out_shape=(result, result, jax.ShapeDtypeStruct((2, *one), F32), jax.ShapeDtypeStruct((2,), jnp.int32)),
         in_specs=[pl.BlockSpec(memory_space=pltpu.HBM)] * 11,
-        out_specs=(pl.BlockSpec(memory_space=VMEM),) * 2,
+        out_specs=(pl.BlockSpec(memory_space=pltpu.HBM),) * 4,
         scratch_shapes=[smem(clips)] * 4
         + [smem(frames), smem(slots)]
         + [VMEM(flat, BF), VMEM(flat, BF), VMEM(conv_weight.shape, BF)]
         + [VMEM(square, BF)] * 4
         + [VMEM((1, channels), F32)] * 2
-        + [VMEM((768, 256), BF), VMEM((128, 256), BF), VMEM((256, 256), BF), VMEM((256, 128), BF), VMEM((256, 256), BF)]
+        + [VMEM((768, 256), BF), VMEM((128, 256), BF), VMEM((256, 256), BF), VMEM((256, 128), BF), VMEM((128, 128), BF)]
         + [
             VMEM(flat, BF),
             VMEM(flat, BF),
@@ -459,26 +509,48 @@
             VMEM((frames + 1, 128, 128), F32),
             VMEM((frames + 1, 128, 128), F32),
             VMEM(flat, BF),
-            VMEM(flat, F32),
         ]
         + [edge, edge]
         + comm()
         + [edge, edge, few, few]
         + comm()
         + [
+            VMEM((frames, 64, 256), F32),
+            VMEM((2, frames, 256), F32),
+            VMEM(flat, BF),
+            VMEM(flat, BF),
+            VMEM((2, *one), F32),
+            smem(2),
             pltpu.SemaphoreType.DMA((11,)),
+            pltpu.SemaphoreType.DMA((4,)),
             pltpu.SemaphoreType.DMA((3, 2)),
             pltpu.SemaphoreType.DMA((3, 2)),
             pltpu.SemaphoreType.DMA((4, 2 * SPAN)),
             pltpu.SemaphoreType.DMA((4, 2 * SPAN)),
         ],
         compiler_params=pltpu.CompilerParams(
-            collective_id=0, has_side_effects=True, vmem_limit_bytes=40 << 20
+            collective_id=0, has_side_effects=True, vmem_limit_bytes=60 << 20
         ),
     )(
         clip_lengths, context_offset, latents.reshape(flat), cotangent.reshape(flat), conv_weight,
         w_query, w_key, w_value, w_out, query_gain.reshape(1, channels), key_gain.reshape(1, channels),
     )
+    out, lg = pl.pallas_call(
+        hand_over,
+        name="hand_over",
+        out_shape=(result, result),
+        in_specs=[pl.BlockSpec(memory_space=pl.ANY)] * 4,
+        out_specs=(pl.BlockSpec(memory_space=pl.ANY),) * 2,
+        scratch_shapes=[
+            VMEM(flat, BF),
+            VMEM(flat, BF),
+            VMEM((2, *one), F32),
+            smem(2),
+            pltpu.SemaphoreType.DMA((4,)),
+            pltpu.SemaphoreType.DMA((2,)),
+        ],
+        compiler_params=pltpu.CompilerParams(vmem_limit_bytes=60 << 20),
+    )(out, lg, pair, spot)
     return out.reshape(latents.shape), lg.reshape(latents.shape)
 
 

time: 37.8 us -> 30.7 us (0.81)
  local copies, waits for them, and re-layouts: 8.33 us -> 0 us
  Pallas kernels: 28.3 us -> 29.9 us
    unnamed x24 -> x0, local copies, waits for them, and re-layouts: 8.33 us -> none
    pallas_call x1 -> x2, Pallas kernels: 28.3 us -> 29.9 us  [the longest x1 27.8 us: per_device(): pl.pallas_call(kernel, name='tokenizer_block', out_shape=(result, result,...]
where the time goes in v1:
time: 30.7 us; the launch traced here: 30.6 us
  Pallas kernels  29.9 us (97%)
  between operations  0.64 us (2%)
    pallas_call x1, Pallas kernels, per_device(): pl.pallas_call(kernel, name='tokenizer_block', out_shape=(result, result,...  27.8 us
    pallas_call x1, Pallas kernels, per_device(): pl.pallas_call(hand_over, name='hand_over', out_shape=(result, result), i...  2.1 us

profile of v1, /device:TPU:24, one launch (start us, length us, event | category | flops | bytes accessed | tf_op | source)
XLA Modules:
  0.0 30.6 jit_solution(5166892735720663594)
XLA Ops:
  0.6 27.8 %tokenizer_block.1 = (bf16[16,128,128]{2,1,0:T(8,128)(2,1)}, bf16[16,128,128]{2,1,0:T(8,128)(2,1)}, f32[2,128,128]{2,1,0:T(8,128)}, s32[2]{0:T(128)}) custom-call(s32[32]{0:T(128)} %lens_h.1, s32[32]{0:T(128)} %offs_h.1, bf16[16,128,128]{2,1,0:T(8,128)(2,1)} %bitcast.6, bf16[16,128,128]{2,1,0:T(8,128)(2,1)} %bitcast.7, bf16[3,3,128,128]{3,2,1,0:T(8,128)(2,1)} %cw_h.1, ...), custom_call_target="tpu_custom_call" | custom-call | tf_op jit(solution)/shard_map/tokenizer_block/pallas_call | solution.py:487
  28.5 2.1 %hand_over.1 = (bf16[16,128,128]{2,1,0:T(8,128)(2,1)}, bf16[16,128,128]{2,1,0:T(8,128)(2,1)}) custom-call(bf16[16,128,128]{2,1,0:T(8,128)(2,1)} %get-tuple-element.8.out_k, bf16[16,128,128]{2,1,0:T(8,128)(2,1)} %get-tuple-element.9.lg_k, f32[2,128,128]{2,1,0:T(8,128)} %get-tuple-element.10.pair_k, s32[2]{0:T(128)} %get-tuple-element.11.spot_k), custom_call_target="tpu_custom_call" | custom-call | tf_op jit(solution)/shard_map/hand_over/pallas_call | solution.py:538
